TPU v7x, 32 devices: a whole 2x2x4 slice. The times are simulated.
32 devices in a mesh: row: 16 (over z, x, core), col: 2 (over y).
Axes of the slice: x: 2, y: 2, z: 4, core: 2. Of those that a mesh axis runs over, the one named last changes fastest.
Arguments:
- blocks: bfloat16 [16, 64, 128, 128], P('row', 'col')
- block_rows: int32 [16, 64], P('row', 'col'), may hold values from 0 to 31, as said below
- block_cols: int32 [16, 64], P('row', 'col'), may hold values from 0 to 31, as said below
- counts: int32 [16, 2], P('row', 'col'), may hold values from 1 to 32, as said below
- trials: bfloat16 [4096, 256], P(('col', 'row')), may hold values from -6 to 6
Outputs:
- basis: float32 [4096, 256], P(('col', 'row'))
- factor: float32 [256, 256], replicated
Inputs may be any that keep to these rules, and one draw needn't show every extreme that they name: The live slots of a device are its first counts[r, c] slots, and at least one device has all 32 slots live. `block_rows`: for the device at grid position (r, c), every slot's block row leaves remainder r on division by the size of axis row. The live slots of a device name distinct blocks with block row at most block column; slots past the count hold arbitrary blocks whose coordinates have the same form. `block_cols`: for the device at grid position (r, c), every slot's block column divided by the size of axis row gives c.
All inputs are finite; a program needn't handle non-finite values.
Results may differ from a plain program's by a relative error of at most 0.0003.
Values may be sent and summed in bfloat16 or wider, within the bound.
A program may use at most 64 MiB of HBM per device.

v0:
```python
import jax
import jax.numpy as jnp
from jax import lax
from jax.sharding import PartitionSpec as P

slot_group = 16


def slot_weights(row_index, col_index, live_from, live_to):
    positions = jnp.arange(row_index.shape[0], dtype=jnp.int32)
    alive = (positions >= live_from) & (positions < live_to)
    return jnp.where(alive, jnp.where(row_index == col_index, 0.5, 1.0), 0.0).astype(jnp.float32)


def spread(weights, places, totals, products):
    for member in range(products.shape[0]):
        totals = totals.at[places[member]].add(weights[member] * products[member])
    return totals


def direct_terms(block_part, vectors, places):
    picked = jnp.take(vectors, places, axis=0)
    return jnp.einsum("sij,sjk->sik", block_part, picked, preferred_element_type=jnp.float32)


def mirror_terms(block_part, vectors, places):
    picked = jnp.take(vectors, places, axis=0)
    return jnp.einsum("sji,sjk->sik", block_part, picked, preferred_element_type=jnp.float32)


def side_slice(values, begin_slot):
    return lax.dynamic_slice_in_dim(values, begin_slot, slot_group, 0)


def sweep(block_set, first_slot, last_slot, accumulate, start_value):
    first_group = first_slot // slot_group
    last_group = (last_slot + slot_group - 1) // slot_group

    def visit_group(group_index, totals):
        begin_slot = group_index * slot_group
        block_part = lax.dynamic_slice_in_dim(block_set, begin_slot, slot_group, 0)
        return accumulate(totals, block_part, begin_slot)

    return lax.fori_loop(first_group, last_group, visit_group, start_value)


def row_side(totals, block_part, begin_slot, weights, row_place, col_place, col_vectors):
    group_rows = side_slice(row_place, begin_slot)
    group_cols = side_slice(col_place, begin_slot)
    products = direct_terms(block_part, col_vectors, group_cols)
    return spread(side_slice(weights, begin_slot), group_rows, totals, products)


def col_side(totals, block_part, begin_slot, weights, row_place, col_place, row_vectors):
    group_rows = side_slice(row_place, begin_slot)
    group_cols = side_slice(col_place, begin_slot)
    products = mirror_terms(block_part, row_vectors, group_rows)
    return spread(side_slice(weights, begin_slot), group_cols, totals, products)


def body(blocks, block_rows, block_cols, counts, trials):
    row_count = lax.axis_size("row")
    col_count = lax.axis_size("col")
    block_edge = trials.shape[0]
    trial_width = trials.shape[1]
    block_set = blocks[0]
    row_index = block_rows[0]
    col_index = block_cols[0]
    live_count = counts[0, 0]
    row_place = row_index // row_count
    col_place = col_index % row_count
    row_vectors = lax.all_gather(trials, "col", axis=0, tiled=True).reshape(
        col_count, block_edge, trial_width
    )
    col_vectors = lax.all_gather(trials, "row", axis=0, tiled=True).reshape(
        row_count, block_edge, trial_width
    )
    row_zero = jnp.zeros((col_count, block_edge, trial_width), jnp.float32)
    col_zero = jnp.zeros((row_count, block_edge, trial_width), jnp.float32)
    weights = slot_weights(row_index, col_index, 0, live_count)

    def both_sides(totals, block_part, begin_slot):
        row_part = row_side(
            totals[0], block_part, begin_slot, weights, row_place, col_place, col_vectors
        )
        col_part = col_side(
            totals[1], block_part, begin_slot, weights, row_place, col_place, row_vectors
        )
        return (row_part, col_part)

    row_part, col_part = sweep(block_set, 0, live_count, both_sides, (row_zero, col_zero))
    row_sum = lax.psum_scatter(
        row_part.reshape(col_count * block_edge, trial_width),
        "col",
        scatter_dimension=0,
        tiled=True,
    )
    col_sum = lax.psum_scatter(
        col_part.reshape(row_count * block_edge, trial_width),
        "row",
        scatter_dimension=0,
        tiled=True,
    )
    products = row_sum + col_sum
    local_gram = jnp.dot(
        products.T, products, precision=lax.Precision.HIGHEST, preferred_element_type=jnp.float32
    )
    gram = lax.psum(local_gram, ("row", "col")) / (row_count * col_count * block_edge)
    lower = jnp.linalg.cholesky(gram)
    basis = jax.scipy.linalg.solve_triangular(lower, products.T, lower=True).T
    return (basis, lower.T)


def solution(mesh):
    return jax.shard_map(
        body,
        mesh=mesh,
        in_specs=(
            P("row", "col", None, None),
            P("row", "col"),
            P("row", "col"),
            P("row", "col"),
            P(("col", "row"), None),
        ),
        out_specs=(P(("col", "row"), None), P()),
        check_vma=False,
    )
```

profile of v0, /device:TPU:0, one launch (start us, length us, event | category | flops | bytes accessed | tf_op | source)
XLA Modules:
  0.0 612.2 jit_solution(9732186749484566758)
XLA Ops:
  8.6 6.1 %all_gather.7 = bf16[256,256]{1,0:T(8,128)(2,1)S(1)} all-gather(bf16[128,256]{1,0:T(8,128)(2,1)} %param.75), channel_id=1, replica_groups=mesh['row'=16,'col'=2] {'col'}, dimensions={0}, use_global_device_ids=true | all-gather | bytes 196608 | tf_op jit(solution)/shard_map/all_gather | solution.py:72
  16.0 1.3 and_select_fusion
  17.2 33.6 %all-gather.2.cloned.1.call-done = bf16[2048,256]{1,0:T(8,128)(2,1)} async-done(((bf16[128,256]{1,0:T(8,128)(2,1)}), bf16[2048,256]{1,0:T(8,128)(2,1)}) %all-gather.2.cloned.1.call-update) | async-done | bytes 1048592 | tf_op jit(solution)/shard_map/all_gather | solution.py:75
  50.9 1.6 broadcast_in_dim.40
  52.5 140.8 %while.45 = (s32[]{:T(128)}, f32[2,128,256]{2,1,0:T(8,128)S(1)}, f32[16,128,256]{2,1,0:T(8,128)}, s32[]{:T(128)}, s32[32]{0:T(128)}, /*index=5*/f32[32]{0:T(128)...) while((s32[]{:T(128)}, f32[2,128,256]{2,1,0:T(8,128)S(1)}, ...), condition=%wide.region_33.34_spmd, body=%wide.region_0.33_spmd.sunk | while | flops 272632608 | bytes 24154408 | solution.py:44
  55.5 1.2 compare_and_fusion.5
  57.3 1.8 gather_fusion
  59.1 1.6 fusion.114
  68.1 1.3 fusion.116
  69.4 1.3 fusion.117
  70.7 1.3 fusion.118
  72.0 1.3 fusion.119
  81.4 1.3 fusion.120
  82.6 1.3 fusion.121
  91.8 1.3 fusion.122
  93.1 1.3 fusion.123
  95.5 1.3 fusion.125
  106.4 1.3 fusion.127
  108.8 1.4 fusion.129
  110.2 1.2 fusion.130
  115.8 1.5 fusion.133
  124.0 2.8 fusion.134
  126.8 2.8 fusion.135
  129.6 2.9 fusion.136
  132.5 2.8 fusion.137
  143.5 2.9 fusion.138
  146.3 2.8 fusion.139
  157.0 2.8 fusion.140
  159.8 2.8 fusion.141
  162.6 2.8 fusion.142
  165.4 2.8 fusion.143
  176.5 2.9 fusion.144
  179.4 2.8 fusion.145
  182.1 2.7 fusion.146
  184.8 2.9 fusion.147
  187.7 2.9 fusion.148
  190.6 2.7 fusion.149
  195.0 149.6 %reduce-scatter.3.cloned.1.call-done = f32[128,256]{1,0:T(8,128)} async-done(((f32[256,256]{1,0:T(8,128)}), f32[128,256]{1,0:T(8,128)}) %reduce-scatter.3.cloned.1.call-update) | async-done | bytes 131088 | tf_op jit(solution)/shard_map/reduce_scatter | solution.py:92
  344.6 65.8 %reduce-scatter.5.cloned.1.call-done = f32[128,256]{1,0:T(8,128)} async-done(((f32[2048,256]{1,0:T(8,128)}), f32[128,256]{1,0:T(8,128)}) %reduce-scatter.5.cloned.1.call-update) | async-done | bytes 131088 | tf_op jit(solution)/shard_map/reduce_scatter | solution.py:98
  410.4 2.2 fusion.56
  413.7 126.8 %all-reduce.3.cloned.1.call-done = f32[256,256]{0,1:T(8,128)} async-done(((f32[256,256]{0,1:T(8,128)}), f32[256,256]{0,1:T(8,128)}) %all-reduce.3.cloned.1.call-update) | async-done | bytes 262160 | tf_op jit(solution)/shard_map/psum | solution.py:108
  542.6 11.7 %cholesky.50 = f32[128,128]{1,0:T(8,128)S(1)} custom-call(f32[128,128]{1,0:T(8,128)S(1)} %cholesky.118), custom_call_target="Cholesky" | custom-call | tf_op jit(solution)/shard_map/jit(cholesky)/cholesky | solution.py:109
  554.4 9.8 %custom-call.15 = f32[1,128,128]{1,2,0:T(8,128)S(1)} custom-call(f32[1,128,128]{2,1,0:T(8,128)S(1)} %get-tuple-element.589), custom_call_target="InvertDiagBlocksLowerTriangular" | custom-call | tf_op jit(solution)/shard_map/jit(cholesky)/cholesky | solution.py:109
  564.7 11.7 %cholesky.105 = f32[128,128]{1,0:T(8,128)S(1)} custom-call(f32[128,128]{1,0:T(8,128)S(1)} %convolution_subtract_fusion.1), custom_call_target="Cholesky" | custom-call | tf_op jit(solution)/shard_map/jit(cholesky)/cholesky | solution.py:109
  579.2 4.3 while.46
  580.0 1.4 bitcast_dynamic-update-slice_fusion.2
  582.1 1.4 bitcast_dynamic-update-slice_fusion.2
  583.5 19.7 %custom-call.16 = f32[2,128,128]{1,2,0:T(8,128)S(1)} custom-call(f32[2,128,128]{2,1,0:T(8,128)S(1)} %get-tuple-element.449), custom_call_target="InvertDiagBlocksLowerTriangular" | custom-call | tf_op jit(solution)/shard_map/jit(_solve_triangular)/triangular_solve | solution.py:110
  (67 shorter events, 27.6 us)
Async XLA Ops:
  7.2 45.3 %copy-start.1 = (s32[3]{0:T(128)S(1)}, s32[3]{0:T(128)}, u32[]{:S(2)}) copy-start(s32[3]{0:T(128)} %constant.793.clone.1) | copy-start | bytes 40
  7.2 45.3 %copy-start.2 = (s32[3]{0:T(128)S(1)}, s32[3]{0:T(128)}, u32[]{:S(2)}) copy-start(s32[3]{0:T(128)} %constant.797.clone.1) | copy-start | bytes 40
  7.2 43.7 %all-gather.2.cloned.1.call-start = ((), (), s32[]{:S(2)}) async-start(), calls=%async_computation.2 | async-start | bytes 1114112 | tf_op jit(solution)/shard_map/all_gather | solution.py:75
  7.9 336.7 %reduce-scatter.3.cloned.1.call-start = ((), (), s32[]{:S(2)}) async-start(), calls=%async_computation.3 | async-start | bytes 393216 | tf_op jit(solution)/shard_map/reduce_scatter | solution.py:92
  59.1 1.6 copy-start.4
  83.9 31.3 %copy-start.3 = (s32[16]{0:T(128)S(1)}, s32[16]{0:T(128)}, u32[]{:S(2)}) copy-start(s32[16]{0:T(128)} %get-tuple-element.818) | copy-start | bytes 196 | tf_op jit(solution)/shard_map/while
  193.3 0.7 copy-start
  194.0 216.4 %reduce-scatter.5.cloned.1.call-start = ((), (), s32[]{:S(2)}) async-start(), calls=%async_computation.4 | async-start | bytes 2228224 | tf_op jit(solution)/shard_map/reduce_scatter | solution.py:98
  194.7 345.7 %all-reduce.3.cloned.1.call-start = ((), (), s32[]{:S(2)}) async-start(), calls=%async_computation.5 | async-start | bytes 524288 | tf_op jit(solution)/shard_map/psum | solution.py:108
Sparse Core Ops, SparseCore 0:
  10.2 40.6 all-gather.1
  194.1 150.4 reduce-scatter.2
  348.8 61.5 reduce-scatter.4
  416.4 124.0 all-reduce.2
where the time goes:
time: 617 us; the launch traced here: 612 us
  waiting for transfers between devices  377 us (61%)
  other arithmetic  134 us (22%)
  loops' own time  59.5 us (10%)
  between operations  15.9 us (3%)
  local copies, waits for them, and re-layouts  12.9 us (2%)
  matrix products  6.65 us (1%)
    reduce_scatter x1, waiting for transfers between devices, body(): lax.psum_scatter(row_part.reshape(col_count * block_edge, trial_width), '...  150 us
    psum x1, waiting for transfers between devices, body(): lax.psum(local_gram, ('row', 'col')) / (row_count * col_count * block_edge)  127 us
    reduce_scatter x1, waiting for transfers between devices, body(): lax.psum_scatter(col_part.reshape(row_count * block_edge, trial_width), '...  65.8 us
    scatter-add x32, other arithmetic, spread(): totals = totals.at[places[member]].add(weights[member] * products[member])  64.8 us
    another operation x1, loops' own time, sweep(): return lax.fori_loop(first_group, last_group, visit_group, start_value)  59.3 us
    another operation x7, other arithmetic, body(): lower = jnp.linalg.cholesky(gram)  34.7 us
    all_gather x1, waiting for transfers between devices, body(): lax.all_gather(trials, 'row', axis=0, tiled=True)  33.6 us
    another operation x2, other arithmetic, body(): basis = jax.scipy.linalg.solve_triangular(lower, products.T, lower=True).T  19.7 us
  transfers between devices with their start and end apart: 4, of which 4 were waited for; matrix products, arithmetic and copies ran while one was open for 1% of the time, Pallas kernels for 0%

commit v1 on v0

v1 whole, which is shorter than its diff:
```python
import functools

import jax
import jax.numpy as jnp
from jax import lax
from jax.experimental import pallas as pl
from jax.experimental.pallas import tpu as pltpu
from jax.sharding import PartitionSpec as P

CORES = 2
DEPTH = 4
PANEL = 32
GROUP = 8
MESH = pl.DeviceIdType.MESH
HIGHEST = lax.Precision.HIGHEST


def products_kernel(
    n_row, n_col, slot_ref, weight_ref, blocks_ref, trials_ref, products_ref, gram_ref,
    row_vec, col_vec, dense, col_part, core_in, side_in, line_in, row_part, col_in,
    gram_part, gram_core, gram_mid, gram_col, gram_all,
    s_vec, r_vec, s_line, r_line, s_side, r_side, s_core, r_core,
    s_pc, r_pc, s_ps, r_ps, s_pl, r_pl, s_pr, r_pr,
    s_gc, r_gc, s_gm, r_gm, s_gy, r_gy, s_ga, r_ga, s_gb, r_gb,
):
    width = n_row // (CORES * DEPTH)
    mids = n_row // CORES
    edge, span = trials_ref.shape
    r, c = lax.axis_index("row"), lax.axis_index("col")
    z, x, k = r // (width * CORES), (r // CORES) % width, r % CORES
    mid = r // CORES
    other = 1 - k

    def at(zz, xx, kk):
        return ((zz * width + xx) * CORES + kk, c)

    core_peer = at(z, x, other)
    mid_peers = [((mid + d) % mids * CORES + k, c) for d in range(1, mids)]
    col_peers = [(r, (c + d) % n_col) for d in range(1, n_col)]

    barrier = pltpu.get_barrier_semaphore()
    for peer in [core_peer, *mid_peers, *col_peers]:
        pl.semaphore_signal(barrier, inc=1, device_id=peer, device_id_type=MESH)
    pl.semaphore_wait(barrier, 1 + len(mid_peers) + len(col_peers))

    def send(src, dst, s_sem, r_sem, peer):
        copy = pltpu.make_async_remote_copy(
            src_ref=src, dst_ref=dst, send_sem=s_sem, recv_sem=r_sem,
            device_id=peer, device_id_type=MESH,
        )
        copy.start()
        return copy

    done = []
    vec_copies = [
        send(trials_ref, row_vec.at[c], s_vec.at[d], r_vec.at[d], peer)
        for d, peer in enumerate(col_peers)
    ]
    line_copies = [
        send(trials_ref, col_vec.at[z, x, k], s_line.at[d - 1], r_line.at[d - 1], at((z + d) % DEPTH, x, k))
        for d in range(1, DEPTH)
    ]
    row_vec[c] = trials_ref[...]
    col_vec[z, x, k] = trials_ref[...]

    def place_cells(b, carry):
        for a in range(n_col):
            cell = a * n_row + b
            w = blocks_ref[slot_ref[cell]].astype(jnp.float32) * weight_ref[cell]
            dense[b, a * edge:(a + 1) * edge, :] = w.astype(jnp.bfloat16)
        return carry

    lax.fori_loop(0, n_row, place_cells, 0)

    for copy in vec_copies:
        copy.wait()
    vectors = row_vec[...].reshape(n_col * edge, span)

    def mirror(zz, xx, kk):
        b = (zz * width + xx) * CORES + kk
        col_part[zz, xx, kk] = lax.dot_general(
            dense[b], vectors, (((0,), (0,)), ((), ())), preferred_element_type=jnp.float32
        )

    order = [(z + 1 + t) % DEPTH for t in range(DEPTH)]
    core_copies = []
    for t in range(DEPTH):
        for xx in range(width):
            mirror(order[t], xx, other)
        core_copies.append(
            send(col_part.at[order[t], :, other], core_in.at[order[t]], s_pc.at[t], r_pc.at[t], core_peer)
        )
    for t in range(DEPTH):
        for xx in range(width):
            mirror(order[t], xx, k)

    for copy in line_copies:
        copy.wait()

    side_copies = []
    for t in range(DEPTH):
        zz = order[t]
        core_copies[t].wait()
        for xx in range(width):
            core_in[zz, xx] = core_in[zz, xx] + col_part[zz, xx, k]
        side_copies.append([
            send(core_in.at[zz, (x + d) % width], side_in.at[d - 1, zz], s_ps.at[t, d - 1], r_ps.at[t, d - 1],
                 at(z, (x + d) % width, k))
            for d in range(1, width)
        ])
    vec_side = [
        send(col_vec.at[:, x, k], col_vec.at[:, x, k], s_side.at[d - 1], r_side.at[d - 1], at(z, (x + d) % width, k))
        for d in range(1, width)
    ]
    tail_copies = []
    for t in range(DEPTH):
        zz = order[t]
        for copy in side_copies[t]:
            copy.wait()
        total = core_in[zz, x]
        for d in range(1, width):
            total = total + side_in[d - 1, zz]
        side_in[0, zz] = total
        if t < DEPTH - 1:
            tail_copies.append(
                send(side_in.at[0, zz], line_in.at[t], s_pl.at[t], r_pl.at[t], at(zz, x, k))
            )
    for copy in vec_side:
        copy.wait()
    vec_core = send(col_vec.at[:, :, k], col_vec.at[:, :, k], s_core, r_core, core_peer)
    vec_core.wait()

    row_part[...] = jnp.zeros_like(row_part)

    def direct(b, carry):
        zz, xx, kk = b // (width * CORES), (b // CORES) % width, b % CORES
        row_part[...] += jnp.dot(
            dense[b], col_vec[zz, xx, kk], preferred_element_type=jnp.float32
        ).reshape(row_part.shape)
        return carry

    lax.fori_loop(0, n_row, direct, 0)
    row_copies = [
        send(row_part.at[(c + d) % n_col], col_in.at[d - 1], s_pr.at[d - 1], r_pr.at[d - 1], col_peers[d - 1])
        for d in range(1, n_col)
    ]
    for copy in tail_copies:
        copy.wait()
    total = side_in[0, z] + row_part[c]
    for d in range(DEPTH - 1):
        total = total + line_in[d]
    for copy in row_copies:
        copy.wait()
    for d in range(n_col - 1):
        total = total + col_in[d]
    products_ref[...] = total

    half, piece = span // CORES, span // n_row
    gram_part[...] = lax.dot_general(
        total, total, (((0,), (0,)), ((), ())), precision=HIGHEST, preferred_element_type=jnp.float32
    ) * (1.0 / (n_row * n_col * edge))
    send(
        gram_part.at[pl.ds(pl.multiple_of(other * half, half), half)], gram_core, s_gc, r_gc, core_peer
    ).wait()
    mine = pl.ds(pl.multiple_of(k * half, half), half)
    gram_core[...] = gram_core[...] + gram_part[mine]

    def rows_of(m):
        return pl.ds(pl.multiple_of(m * piece, piece), piece)

    mid_copies = [
        send(gram_core.at[rows_of((mid + d) % mids)], gram_mid.at[d - 1], s_gm.at[d - 1], r_gm.at[d - 1], mid_peers[d - 1])
        for d in range(1, mids)
    ]
    total = gram_core[rows_of(mid)]
    for d in range(1, mids):
        mid_copies[d - 1].wait()
        total = total + gram_mid[d - 1]
    gram_col[c] = total
    col_copies = [
        send(gram_col.at[c], gram_col.at[c], s_gy.at[d - 1], r_gy.at[d - 1], col_peers[d - 1])
        for d in range(1, n_col)
    ]
    for copy in col_copies:
        copy.wait()
    total = gram_col[0]
    for d in range(1, n_col):
        total = total + gram_col[d]
    own = pl.ds(pl.multiple_of(k * half + mid * piece, piece), piece)
    gram_all[own] = total
    back = [
        send(gram_all.at[own], gram_all.at[own], s_ga.at[d - 1], r_ga.at[d - 1], mid_peers[d - 1])
        for d in range(1, mids)
    ]
    for copy in back:
        copy.wait()
    send(gram_all.at[mine], gram_all.at[mine], s_gb, r_gb, core_peer).wait()
    gram_ref[...] = gram_all[...]


def factor_kernel(gram_ref, products_ref, basis_ref, factor_ref, work):
    span = gram_ref.shape[0]
    rows_all = lax.broadcasted_iota(jnp.int32, (span, span), 0)
    cols_all = lax.broadcasted_iota(jnp.int32, (span, span), 1)
    work[:, :span] = gram_ref[...]
    work[:, span:] = jnp.where(rows_all == cols_all, 1.0, 0.0).astype(jnp.float32)
    place = lax.broadcasted_iota(jnp.int32, (PANEL, 128), 0)
    tiles = 2 * span // 128
    for first in range(0, span, PANEL):
        base = first // 128 * 128
        last_tile = (span + first + PANEL + 127) // 128
        live = [t for t in range(tiles) if first // 128 <= t < last_tile]
        part = {t: work[first:first + PANEL, t * 128:(t + 1) * 128] for t in live}
        scale = jnp.ones((PANEL, 128), jnp.float32)
        for start in range(0, PANEL, GROUP):
            lane = first + start - base
            lead = part[first // 128]
            cols = [
                jnp.broadcast_to(lead[:, lane + m:lane + m + 1], (PANEL, 128)) for m in range(GROUP)
            ]
            for m in range(GROUP):
                at = start + m
                pivot = cols[m][at:at + 1]
                root = lax.rsqrt(pivot)
                root = root * (1.5 - 0.5 * pivot * root * root)
                inverse = root * root
                below = jnp.where(place > at, cols[m], 0.0)
                for other in range(m + 1, GROUP):
                    cols[other] = cols[other] - below * (cols[other][at:at + 1] * inverse)
                for t in live:
                    part[t] = part[t] - below * (part[t][at:at + 1] * inverse)
                scale = jnp.where(place == at, root, scale)
        for t in live:
            part[t] = part[t] * scale
            work[first:first + PANEL, t * 128:(t + 1) * 128] = part[t]
        after = first + PANEL
        if after < span:
            low = after // 128
            left = jnp.concatenate([part[t] for t in range(low, span // 128)], axis=1)
            right = jnp.concatenate([part[t] for t in range(low, last_tile)], axis=1)
            change = lax.dot_general(
                left, right, (((0,), (0,)), ((), ())), precision=HIGHEST, preferred_element_type=jnp.float32
            )
            work[after:, low * 128:last_tile * 128] -= change[after - low * 128:]
    factor_ref[...] = jnp.where(rows_all <= cols_all, work[:, :span], 0.0)
    basis_ref[...] = lax.dot_general(
        products_ref[...], work[:, span:], (((1,), (1,)), ((), ())),
        precision=HIGHEST, preferred_element_type=jnp.float32,
    )


def body(blocks, block_rows, block_cols, counts, trials):
    n_row, n_col = lax.axis_size("row"), lax.axis_size("col")
    width, mids = n_row // (CORES * DEPTH), n_row // CORES
    edge, span = trials.shape
    row_index, col_index = block_rows[0], block_cols[0]
    cells = n_row * n_col
    slots = row_index.shape[0]
    spots = row_index // n_row * n_row + col_index % n_row
    position = jnp.arange(slots, dtype=jnp.int32)
    held = (spots[None, :] == jnp.arange(cells, dtype=jnp.int32)[:, None]) & (position < counts[0, 0])[None, :]
    slot = jnp.sum(jnp.where(held, position[None, :], 0), axis=1)
    weight = jnp.sum(
        jnp.where(held, jnp.where(row_index == col_index, 0.5, 1.0)[None, :], 0.0), axis=1
    ).astype(jnp.float32)

    vmem = pl.BlockSpec(memory_space=pltpu.VMEM)
    smem = pl.BlockSpec(memory_space=pltpu.SMEM)
    f32, bf16 = jnp.float32, jnp.bfloat16
    dma = pltpu.SemaphoreType.DMA
    side = max(width - 1, 1)

    def pair(shape=()):
        return [dma(shape) if shape else dma, dma(shape) if shape else dma]

    products, gram = pl.pallas_call(
        functools.partial(products_kernel, n_row, n_col),
        out_shape=(
            jax.ShapeDtypeStruct((edge, span), f32),
            jax.ShapeDtypeStruct((span, span), f32),
        ),
        in_specs=[smem, smem, vmem, vmem],
        out_specs=(vmem, vmem),
        scratch_shapes=[
            pltpu.VMEM((n_col, edge, span), bf16),
            pltpu.VMEM((DEPTH, width, CORES, edge, span), bf16),
            pltpu.VMEM((n_row, n_col * edge, edge), bf16),
            pltpu.VMEM((DEPTH, width, CORES, edge, span), f32),
            pltpu.VMEM((DEPTH, width, edge, span), f32),
            pltpu.VMEM((side, DEPTH, edge, span), f32),
            pltpu.VMEM((DEPTH - 1, edge, span), f32),
            pltpu.VMEM((n_col, edge, span), f32),
            pltpu.VMEM((n_col - 1, edge, span), f32),
            pltpu.VMEM((span, span), f32),
            pltpu.VMEM((span // CORES, span), f32),
            pltpu.VMEM((mids - 1, span // n_row, span), f32),
            pltpu.VMEM((n_col, span // n_row, span), f32),
            pltpu.VMEM((span, span), f32),
            *pair((n_col - 1,)), *pair((DEPTH - 1,)), *pair((side,)), *pair(),
            *pair((DEPTH,)), *pair((DEPTH, side)), *pair((DEPTH - 1,)), *pair((n_col - 1,)),
            *pair(), *pair((mids - 1,)), *pair((n_col - 1,)), *pair((mids - 1,)), *pair(),
        ],
        compiler_params=pltpu.CompilerParams(
            collective_id=0, has_side_effects=True, vmem_limit_bytes=48 * 1024 * 1024
        ),
        name="products",
    )(slot, weight, blocks[0], trials)

    basis, factor = pl.pallas_call(
        factor_kernel,
        out_shape=(
            jax.ShapeDtypeStruct((edge, span), f32),
            jax.ShapeDtypeStruct((span, span), f32),
        ),
        in_specs=[vmem, vmem],
        out_specs=(vmem, vmem),
        scratch_shapes=[pltpu.VMEM((span, 2 * span), f32)],
        compiler_params=pltpu.CompilerParams(vmem_limit_bytes=32 * 1024 * 1024),
        name="factorize",
    )(gram, products)
    return basis, factor


def solution(mesh):
    return jax.shard_map(
        body,
        mesh=mesh,
        in_specs=(
            P("row", "col", None, None),
            P("row", "col"),
            P("row", "col"),
            P("row", "col"),
            P(("col", "row"), None),
        ),
        out_specs=(P(("col", "row"), None), P()),
        check_vma=False,
    )
```

time: 617 us -> 71.8 us (0.12)
  waiting for transfers between devices: 377 us -> 0 us
  other arithmetic: 134 us -> 0.25 us
  Pallas kernels: 0 us -> 67.3 us
  loops' own time: 59.5 us -> 0 us
  between operations: 15.9 us -> 1.33 us
  local copies, waits for them, and re-layouts: 12.9 us -> 2.72 us
  matrix products: 6.65 us -> 0 us
    reduce_scatter x2 -> x0, waiting for transfers between devices: 215 us -> none  [the longest x1 150 us: body(): lax.psum_scatter(row_part.reshape(col_count * block_edge, trial_width), '...]
    psum x1 -> x0, waiting for transfers between devices: 127 us -> none  [body(): lax.psum(local_gram, ('row', 'col')) / (row_count * col_count * block_edge)]
    pallas_call x0 -> x2, Pallas kernels: none -> 67.3 us  [the longest x1 56.4 us: body(): pl.pallas_call(functools.partial(products_kernel, n_row, n_col), out_shap...]
    scatter-add x32 -> x0, other arithmetic: 64.8 us -> none  [spread(): totals = totals.at[places[member]].add(weights[member] * products[member])]
    another operation x17 -> x0, other arithmetic: 60.8 us -> none  [the longest x7 34.7 us: body(): lower = jnp.linalg.cholesky(gram)]
    another operation x2 -> x0, loops' own time: 59.5 us -> none  [the longest x1 59.3 us: sweep(): return lax.fori_loop(first_group, last_group, visit_group, start_value)]
    all_gather x1 -> x0, waiting for transfers between devices: 33.6 us -> none  [body(): lax.all_gather(trials, 'row', axis=0, tiled=True)]
  transfers between devices with their start and end apart: 4 -> 0, of which waited for: 4 -> 0; matrix products, arithmetic and copies ran while one was open for 1% -> 0% of each run, Pallas kernels for 0% -> 0%
where the time goes in v1:
time: 71.8 us; the launch traced here: 71.6 us
  Pallas kernels  67.3 us (94%)
  local copies, waits for them, and re-layouts  2.72 us (4%)
  between operations  1.33 us (2%)
    pallas_call x1, Pallas kernels, body(): pl.pallas_call(functools.partial(products_kernel, n_row, n_col), out_shap...  56.4 us
    pallas_call x1, Pallas kernels, body(): pl.pallas_call(factor_kernel, out_shape=(jax.ShapeDtypeStruct((edge, span...  11 us
    unnamed x8, local copies, waits for them, and re-layouts  2.72 us

profile of v1, /device:TPU:0, one launch (start us, length us, event | category | flops | bytes accessed | tf_op | source)
XLA Modules:
  0.0 71.6 jit_solution(15233576710800964462)
XLA Ops:
  1.3 0.0 copy-start.2
  1.3 0.0 copy-start.3
  1.3 0.6 copy-done.2
  1.9 0.0 copy-done.3
  2.0 0.1 select_reduce_fusion.1.slot_ref
  2.1 0.1 select_reduce_fusion.weight_ref
  2.2 0.0 copy-start
  2.2 1.2 %copy-done = bf16[1,32,128,128]{3,2,1,0:T(8,128)(2,1)S(1)} copy-done((bf16[1,32,128,128]{3,2,1,0:T(8,128)(2,1)S(1)}, bf16[1,32,128,128]{3,2,1,0:T(8,128)(2,1)}, u32[]{:S(2)}) %copy-start) | copy-done | bytes 1048600
  3.4 0.0 copy-start.1
  3.5 0.8 %copy-done.1 = bf16[128,256]{1,0:T(8,128)(2,1)S(1)} copy-done((bf16[128,256]{1,0:T(8,128)(2,1)S(1)}, bf16[128,256]{1,0:T(8,128)(2,1)}, u32[]{:S(2)}) %copy-start.1) | copy-done | bytes 65560
  4.3 56.4 %products.1 = (f32[128,256]{1,0:T(8,128)S(1)}, f32[256,256]{1,0:T(8,128)S(1)}) custom-call(s32[32]{0:T(128)S(1)} %select_reduce_fusion.1.slot_ref, f32[32]{0:T(128)S(1)} %select_reduce_fusion.weight_ref, bf16[32,128,128]{2,1,0:T(8,128)(2,1)S(1)} %bitcast.7, bf16[128,256]{1,0:T(8,128)(2,1)S(1)} %copy-done.1), custom_call_target="tpu_custom_call" | custom-call | tf_op jit(solution)/shard_map/products/pallas_call | solution.py:276
  60.6 11.0 %factorize.1 = (f32[128,256]{1,0:T(8,128)}, f32[256,256]{1,0:T(8,128)}) custom-call(f32[256,256]{1,0:T(8,128)S(1)} %get-tuple-element.4.gram_ref, f32[128,256]{1,0:T(8,128)S(1)} %get-tuple-element.5.products_ref), custom_call_target="tpu_custom_call" | custom-call | tf_op jit(solution)/shard_map/factorize/pallas_call | solution.py:309
  (3 shorter events, 0.0 us)
Async XLA Ops:
  1.3 0.7 copy-start.2
  1.3 0.7 copy-start.3
  2.2 1.2 %copy-start = (bf16[1,32,128,128]{3,2,1,0:T(8,128)(2,1)S(1)}, bf16[1,32,128,128]{3,2,1,0:T(8,128)(2,1)}, u32[]{:S(2)}) copy-start(bf16[1,32,128,128]{3,2,1,0:T(8,128)(2,1)} %param.5) | copy-start | bytes 3145732
  3.4 0.8 %copy-start.1 = (bf16[128,256]{1,0:T(8,128)(2,1)S(1)}, bf16[128,256]{1,0:T(8,128)(2,1)}, u32[]{:S(2)}) copy-start(bf16[128,256]{1,0:T(8,128)(2,1)} %trials_ref.1) | copy-start | bytes 196612

commit v2 on v1

--- a/solution.py
+++ b/solution.py
@@ -16,16 +16,19 @@
 
 
 def products_kernel(
-    n_row, n_col, slot_ref, weight_ref, blocks_ref, trials_ref, products_ref, gram_ref,
-    row_vec, col_vec, dense, col_part, core_in, side_in, line_in, row_part, col_in,
-    gram_part, gram_core, gram_mid, gram_col, gram_all,
+    n_row, n_col, info_ref, blocks_ref, trials_ref, products_ref, gram_ref,
+    held, row_vec, col_vec, dense, col_part, core_in, side_in, line_in, row_part, col_in,
+    gram_part, gram_core, gram_mid, gram_col, gram_all, held_sem,
     s_vec, r_vec, s_line, r_line, s_side, r_side, s_core, r_core,
     s_pc, r_pc, s_ps, r_ps, s_pl, r_pl, s_pr, r_pr,
     s_gc, r_gc, s_gm, r_gm, s_gy, r_gy, s_ga, r_ga, s_gb, r_gb,
 ):
     width = n_row // (CORES * DEPTH)
     mids = n_row // CORES
+    cells = n_row * n_col
     edge, span = trials_ref.shape
+    load = pltpu.make_async_copy(blocks_ref, held, held_sem)
+    load.start()
     r, c = lax.axis_index("row"), lax.axis_index("col")
     z, x, k = r // (width * CORES), (r // CORES) % width, r % CORES
     mid = r // CORES
@@ -41,6 +44,20 @@
     barrier = pltpu.get_barrier_semaphore()
     for peer in [core_peer, *mid_peers, *col_peers]:
         pl.semaphore_signal(barrier, inc=1, device_id=peer, device_id_type=MESH)
+
+    def columns(b):
+        return pl.ds(pl.multiple_of(b * edge, edge), edge)
+
+    def place_cells(b, carry):
+        for a in range(n_col):
+            cell = a * n_row + b
+            weight = info_ref[cells + cell].astype(jnp.float32) * 0.5
+            w = held[info_ref[cell]].astype(jnp.float32) * weight
+            dense[a * edge:(a + 1) * edge, columns(b)] = w.astype(jnp.bfloat16)
+        return carry
+
+    load.wait()
+    lax.fori_loop(0, n_row // 2, place_cells, 0)
     pl.semaphore_wait(barrier, 1 + len(mid_peers) + len(col_peers))
 
     def send(src, dst, s_sem, r_sem, peer):
@@ -51,7 +68,6 @@
         copy.start()
         return copy
 
-    done = []
     vec_copies = [
         send(trials_ref, row_vec.at[c], s_vec.at[d], r_vec.at[d], peer)
         for d, peer in enumerate(col_peers)
@@ -62,15 +78,7 @@
     ]
     row_vec[c] = trials_ref[...]
     col_vec[z, x, k] = trials_ref[...]
-
-    def place_cells(b, carry):
-        for a in range(n_col):
-            cell = a * n_row + b
-            w = blocks_ref[slot_ref[cell]].astype(jnp.float32) * weight_ref[cell]
-            dense[b, a * edge:(a + 1) * edge, :] = w.astype(jnp.bfloat16)
-        return carry
-
-    lax.fori_loop(0, n_row, place_cells, 0)
+    lax.fori_loop(n_row // 2, n_row, place_cells, 0)
 
     for copy in vec_copies:
         copy.wait()
@@ -79,7 +87,7 @@
     def mirror(zz, xx, kk):
         b = (zz * width + xx) * CORES + kk
         col_part[zz, xx, kk] = lax.dot_general(
-            dense[b], vectors, (((0,), (0,)), ((), ())), preferred_element_type=jnp.float32
+            dense[:, columns(b)], vectors, (((0,), (0,)), ((), ())), preferred_element_type=jnp.float32
         )
 
     order = [(z + 1 + t) % DEPTH for t in range(DEPTH)]
@@ -94,9 +102,6 @@
         for xx in range(width):
             mirror(order[t], xx, k)
 
-    for copy in line_copies:
-        copy.wait()
-
     side_copies = []
     for t in range(DEPTH):
         zz = order[t]
@@ -108,10 +113,15 @@
                  at(z, (x + d) % width, k))
             for d in range(1, width)
         ])
-    vec_side = [
-        send(col_vec.at[:, x, k], col_vec.at[:, x, k], s_side.at[d - 1], r_side.at[d - 1], at(z, (x + d) % width, k))
-        for d in range(1, width)
-    ]
+        if t == 0:
+            for copy in line_copies:
+                copy.wait()
+            vec_side = [
+                send(col_vec.at[:, x, k], col_vec.at[:, x, k], s_side.at[d - 1], r_side.at[d - 1],
+                     at(z, (x + d) % width, k))
+                for d in range(1, width)
+            ]
+
     tail_copies = []
     for t in range(DEPTH):
         zz = order[t]
@@ -125,48 +135,56 @@
             tail_copies.append(
                 send(side_in.at[0, zz], line_in.at[t], s_pl.at[t], r_pl.at[t], at(zz, x, k))
             )
-    for copy in vec_side:
-        copy.wait()
-    vec_core = send(col_vec.at[:, :, k], col_vec.at[:, :, k], s_core, r_core, core_peer)
-    vec_core.wait()
-
-    row_part[...] = jnp.zeros_like(row_part)
-
-    def direct(b, carry):
-        zz, xx, kk = b // (width * CORES), (b // CORES) % width, b % CORES
-        row_part[...] += jnp.dot(
-            dense[b], col_vec[zz, xx, kk], preferred_element_type=jnp.float32
-        ).reshape(row_part.shape)
-        return carry
-
-    lax.fori_loop(0, n_row, direct, 0)
-    row_copies = [
-        send(row_part.at[(c + d) % n_col], col_in.at[d - 1], s_pr.at[d - 1], r_pr.at[d - 1], col_peers[d - 1])
-        for d in range(1, n_col)
-    ]
-    for copy in tail_copies:
-        copy.wait()
+        if t == 0:
+            for copy in vec_side:
+                copy.wait()
+            vec_core = send(col_vec.at[:, :, k], col_vec.at[:, :, k], s_core, r_core, core_peer)
+        if t == 1:
+            vec_core.wait()
+            group = width * CORES * edge
+            acc = jnp.zeros((n_col * edge, span), jnp.float32)
+            for part in range(DEPTH):
+                acc = acc + jnp.dot(
+                    dense[:, part * group:(part + 1) * group], col_vec[part].reshape(group, span),
+                    preferred_element_type=jnp.float32,
+                )
+            row_part[...] = acc.reshape(row_part.shape)
+            row_copies = [
+                send(row_part.at[(c + d) % n_col], col_in.at[d - 1], s_pr.at[d - 1], r_pr.at[d - 1], col_peers[d - 1])
+                for d in range(1, n_col)
+            ]
     total = side_in[0, z] + row_part[c]
-    for d in range(DEPTH - 1):
-        total = total + line_in[d]
     for copy in row_copies:
         copy.wait()
     for d in range(n_col - 1):
         total = total + col_in[d]
+    for d in range(DEPTH - 1):
+        tail_copies[d].wait()
+        total = total + line_in[d]
     products_ref[...] = total
 
-    half, piece = span // CORES, span // n_row
-    gram_part[...] = lax.dot_general(
-        total, total, (((0,), (0,)), ((), ())), precision=HIGHEST, preferred_element_type=jnp.float32
-    ) * (1.0 / (n_row * n_col * edge))
+    quarter, piece = span // 2, gram_mid.shape[1]
+    half = piece * mids
+    left, right = total[:, :quarter], total[:, quarter:]
+
+    def inner(a, b):
+        return lax.dot_general(
+            a, b, (((0,), (0,)), ((), ())), precision=HIGHEST, preferred_element_type=jnp.float32
+        ) * (1.0 / (n_row * n_col * edge))
+
+    if gram_part.shape[0] > 3 * quarter:
+        gram_part[3 * quarter:] = jnp.zeros((gram_part.shape[0] - 3 * quarter, quarter), jnp.float32)
+    gram_part[:quarter] = inner(left, left)
+    gram_part[quarter:2 * quarter] = inner(left, right)
+    gram_part[2 * quarter:3 * quarter] = inner(right, right)
     send(
-        gram_part.at[pl.ds(pl.multiple_of(other * half, half), half)], gram_core, s_gc, r_gc, core_peer
+        gram_part.at[pl.ds(pl.multiple_of(other * half, 8), half)], gram_core, s_gc, r_gc, core_peer
     ).wait()
-    mine = pl.ds(pl.multiple_of(k * half, half), half)
+    mine = pl.ds(pl.multiple_of(k * half, 8), half)
     gram_core[...] = gram_core[...] + gram_part[mine]
 
     def rows_of(m):
-        return pl.ds(pl.multiple_of(m * piece, piece), piece)
+        return pl.ds(pl.multiple_of(m * piece, 8), piece)
 
     mid_copies = [
         send(gram_core.at[rows_of((mid + d) % mids)], gram_mid.at[d - 1], s_gm.at[d - 1], r_gm.at[d - 1], mid_peers[d - 1])
@@ -186,7 +204,7 @@
     total = gram_col[0]
     for d in range(1, n_col):
         total = total + gram_col[d]
-    own = pl.ds(pl.multiple_of(k * half + mid * piece, piece), piece)
+    own = pl.ds(pl.multiple_of(k * half + mid * piece, 8), piece)
     gram_all[own] = total
     back = [
         send(gram_all.at[own], gram_all.at[own], s_ga.at[d - 1], r_ga.at[d - 1], mid_peers[d - 1])
@@ -195,14 +213,18 @@
     for copy in back:
         copy.wait()
     send(gram_all.at[mine], gram_all.at[mine], s_gb, r_gb, core_peer).wait()
-    gram_ref[...] = gram_all[...]
+    gram_ref[...] = gram_all[:3 * quarter]
 
 
 def factor_kernel(gram_ref, products_ref, basis_ref, factor_ref, work):
-    span = gram_ref.shape[0]
+    span = work.shape[0]
     rows_all = lax.broadcasted_iota(jnp.int32, (span, span), 0)
     cols_all = lax.broadcasted_iota(jnp.int32, (span, span), 1)
-    work[:, :span] = gram_ref[...]
+    quarter = span // 2
+    work[:quarter, :quarter] = gram_ref[:quarter]
+    work[:quarter, quarter:span] = gram_ref[quarter:span]
+    work[quarter:, quarter:span] = gram_ref[span:]
+    work[quarter:, :quarter] = jnp.zeros((quarter, quarter), jnp.float32)
     work[:, span:] = jnp.where(rows_all == cols_all, 1.0, 0.0).astype(jnp.float32)
     place = lax.broadcasted_iota(jnp.int32, (PANEL, 128), 0)
     tiles = 2 * span // 128
@@ -259,16 +281,16 @@
     spots = row_index // n_row * n_row + col_index % n_row
     position = jnp.arange(slots, dtype=jnp.int32)
     held = (spots[None, :] == jnp.arange(cells, dtype=jnp.int32)[:, None]) & (position < counts[0, 0])[None, :]
-    slot = jnp.sum(jnp.where(held, position[None, :], 0), axis=1)
-    weight = jnp.sum(
-        jnp.where(held, jnp.where(row_index == col_index, 0.5, 1.0)[None, :], 0.0), axis=1
-    ).astype(jnp.float32)
+    twice = jnp.where(row_index == col_index, 1, 2).astype(jnp.int32)
+    marks = jnp.stack([position, twice])
+    info = jnp.sum(jnp.where(held[None], marks[:, None, :], 0), axis=2).reshape(2 * cells)
 
     vmem = pl.BlockSpec(memory_space=pltpu.VMEM)
     smem = pl.BlockSpec(memory_space=pltpu.SMEM)
     f32, bf16 = jnp.float32, jnp.bfloat16
     dma = pltpu.SemaphoreType.DMA
     side = max(width - 1, 1)
+    piece = (3 * span // 2 + 8 * n_row - 1) // (8 * n_row) * 8
 
     def pair(shape=()):
         return [dma(shape) if shape else dma, dma(shape) if shape else dma]
@@ -277,34 +299,36 @@
         functools.partial(products_kernel, n_row, n_col),
         out_shape=(
             jax.ShapeDtypeStruct((edge, span), f32),
-            jax.ShapeDtypeStruct((span, span), f32),
+            jax.ShapeDtypeStruct((3 * span // 2, span // 2), f32),
         ),
-        in_specs=[smem, smem, vmem, vmem],
+        in_specs=[smem, pl.BlockSpec(memory_space=pltpu.HBM), vmem],
         out_specs=(vmem, vmem),
         scratch_shapes=[
+            pltpu.VMEM((slots, edge, edge), bf16),
             pltpu.VMEM((n_col, edge, span), bf16),
             pltpu.VMEM((DEPTH, width, CORES, edge, span), bf16),
-            pltpu.VMEM((n_row, n_col * edge, edge), bf16),
+            pltpu.VMEM((n_col * edge, n_row * edge), bf16),
             pltpu.VMEM((DEPTH, width, CORES, edge, span), f32),
             pltpu.VMEM((DEPTH, width, edge, span), f32),
             pltpu.VMEM((side, DEPTH, edge, span), f32),
             pltpu.VMEM((DEPTH - 1, edge, span), f32),
             pltpu.VMEM((n_col, edge, span), f32),
             pltpu.VMEM((n_col - 1, edge, span), f32),
-            pltpu.VMEM((span, span), f32),
-            pltpu.VMEM((span // CORES, span), f32),
-            pltpu.VMEM((mids - 1, span // n_row, span), f32),
-            pltpu.VMEM((n_col, span // n_row, span), f32),
-            pltpu.VMEM((span, span), f32),
+            pltpu.VMEM((piece * n_row, span // 2), f32),
+            pltpu.VMEM((piece * mids, span // 2), f32),
+            pltpu.VMEM((mids - 1, piece, span // 2), f32),
+            pltpu.VMEM((n_col, piece, span // 2), f32),
+            pltpu.VMEM((piece * n_row, span // 2), f32),
+            dma,
             *pair((n_col - 1,)), *pair((DEPTH - 1,)), *pair((side,)), *pair(),
             *pair((DEPTH,)), *pair((DEPTH, side)), *pair((DEPTH - 1,)), *pair((n_col - 1,)),
             *pair(), *pair((mids - 1,)), *pair((n_col - 1,)), *pair((mids - 1,)), *pair(),
         ],
         compiler_params=pltpu.CompilerParams(
-            collective_id=0, has_side_effects=True, vmem_limit_bytes=48 * 1024 * 1024
+            collective_id=0, has_side_effects=True, vmem_limit_bytes=60 * 1024 * 1024
         ),
         name="products",
-    )(slot, weight, blocks[0], trials)
+    )(info, blocks[0], trials)
 
     basis, factor = pl.pallas_call(
         factor_kernel,

time: 71.8 us -> 65.3 us (0.909)
  Pallas kernels: 67.3 us -> 60.5 us
    pallas_call x1, Pallas kernels: 56.4 us -> 49.5 us  [body(): pl.pallas_call(functools.partial(products_kernel, n_row, n_col), out_shap...]
where the time goes in v2:
time: 65.3 us; the launch traced here: 65.1 us
  Pallas kernels  60.5 us (93%)
  local copies, waits for them, and re-layouts  3.07 us (5%)
  between operations  1.34 us (2%)
    pallas_call x1, Pallas kernels, body(): pl.pallas_call(functools.partial(products_kernel, n_row, n_col), out_shap...  49.5 us
    pallas_call x1, Pallas kernels, body(): pl.pallas_call(factor_kernel, out_shape=(jax.ShapeDtypeStruct((edge, span...  11 us
    unnamed x8, local copies, waits for them, and re-layouts  2.47 us

profile of v2, /device:TPU:0, one launch (start us, length us, event | category | flops | bytes accessed | tf_op | source)
XLA Modules:
  0.0 65.1 jit_solution(10907791236158749881)
XLA Ops:
  1.3 0.0 copy-start.2
  1.3 0.0 copy-start.3
  1.3 0.6 copy-done.2
  1.9 0.0 copy-done.3
  2.0 0.1 select_reduce_fusion
  2.1 0.6 reshape.49.info_ref
  2.7 49.5 %products.1 = (f32[128,256]{1,0:T(8,128)}, f32[384,128]{1,0:T(8,128)}) custom-call(s32[64]{0:T(128)} %reshape.49.info_ref, bf16[32,128,128]{2,1,0:T(8,128)(2,1)} %bitcast.5, bf16[128,256]{1,0:T(8,128)(2,1)} %trials_ref.1), custom_call_target="tpu_custom_call" | custom-call | tf_op jit(solution)/shard_map/products/pallas_call | solution.py:298
  52.2 0.0 copy-start
  52.3 0.9 %copy-done = f32[384,128]{1,0:T(8,128)S(1)} copy-done((f32[384,128]{1,0:T(8,128)S(1)}, f32[384,128]{1,0:T(8,128)}, u32[]{:S(2)}) %copy-start) | copy-done | bytes 196632
  53.2 0.0 copy-start.1
  53.2 0.9 %copy-done.1 = f32[128,256]{1,0:T(8,128)S(1)} copy-done((f32[128,256]{1,0:T(8,128)S(1)}, f32[128,256]{1,0:T(8,128)}, u32[]{:S(2)}) %copy-start.1) | copy-done | bytes 131096
  54.1 11.0 %factorize.1 = (f32[128,256]{1,0:T(8,128)}, f32[256,256]{1,0:T(8,128)}) custom-call(f32[384,128]{1,0:T(8,128)S(1)} %copy-done, f32[128,256]{1,0:T(8,128)S(1)} %copy-done.1), custom_call_target="tpu_custom_call" | custom-call | tf_op jit(solution)/shard_map/factorize/pallas_call | solution.py:333
  (5 shorter events, 0.0 us)
Async XLA Ops:
  1.3 0.7 %copy-start.2 = (s32[1,32]{1,0:T(1,128)S(1)}, s32[1,32]{1,0:T(1,128)}, u32[]{:S(2)}) copy-start(s32[1,32]{1,0:T(1,128)} %param.7) | copy-start | bytes 388
  1.3 0.7 %copy-start.3 = (s32[1,32]{1,0:T(1,128)S(1)}, s32[1,32]{1,0:T(1,128)}, u32[]{:S(2)}) copy-start(s32[1,32]{1,0:T(1,128)} %param.6) | copy-start | bytes 388
  52.2 0.9 %copy-start = (f32[384,128]{1,0:T(8,128)S(1)}, f32[384,128]{1,0:T(8,128)}, u32[]{:S(2)}) copy-start(f32[384,128]{1,0:T(8,128)} %get-tuple-element.4.gram_ref) | copy-start | bytes 589828
  53.2 0.9 %copy-start.1 = (f32[128,256]{1,0:T(8,128)S(1)}, f32[128,256]{1,0:T(8,128)}, u32[]{:S(2)}) copy-start(f32[128,256]{1,0:T(8,128)} %get-tuple-element.5.products_ref) | copy-start | bytes 393220
